TPU v7x, 512 devices: a whole 4x8x8 slice. The times are simulated.
512 devices in a mesh: tm: 64 (over x, z, core), region: 8 (over y).
Axes of the slice: x: 4, y: 8, z: 8, core: 2. Of those that a mesh axis runs over, the one named last changes fastest.
Arguments:
- activity: bfloat16 [6144, 131072], P('region', 'tm'), may hold values from -6 to 6
- test_matrix: bfloat16 [131072, 512], P('tm', 'region'), may hold values from -0.015625 to 0.015625
- basis_mix: float32 [512, 64], replicated, may hold values from -0.25 to 0.25
- recurrent: float32 [64, 64], replicated, may hold values from -0.75 to 0.75
- latent_bias: float32 [64], replicated, may hold values from -2 to 2
- readout: bfloat16 [6144, 64], P('region'), may hold values from -0.75 to 0.75
- region_in: bfloat16 [6144, 8], P('region'), may hold values from -0.21875 to 0.21875
- region_out: bfloat16 [6144, 8], P('region'), may hold values from -1 to 1
- region_of_block: int32 [48], replicated, may hold values from 0 to 7, never falling along the last dimension, each value on 1 to 12 neighbouring positions
- region_mask: int32 [8, 8], replicated, may hold values 0 or 1
Outputs:
- latents: float32 [64, 131072], P(None, 'tm')
- frame_loss: float32 [131072], P('tm')
- readout_score: float32 [6144, 64], P('region')
Inputs may be any that keep to these rules, and one draw needn't show every extreme that they name: `region_of_block`: blocks of one region are consecutive, every region holds at least one block, and no region holds more than 12 blocks.
All inputs are finite; a program needn't handle non-finite values.
Results may differ from a plain program's by a relative error of at most 0.0028.
Values may be sent and summed in bfloat16 or wider, within the bound.
No kernel may reach another device: no remote copies, remote signals or barrier semaphores. Data moves between devices by JAX's collectives and lax.ppermute only.
A program may use at most 64 MiB of HBM per device.

v0:
```python
import jax
import jax.numpy as jnp
from jax import lax
from jax.sharding import PartitionSpec as P

BLOCK = 128
precise = lax.Precision.HIGHEST
epsilon = 1e-05


def from_behind(block, axis, distance):
    devices = range(lax.axis_size(axis))
    route = [(i - distance, i) for i in devices if i - distance in devices]
    return lax.ppermute(block, axis, route)


def orthonormal(sketch, gram):
    lower = jnp.linalg.cholesky(gram)
    return jax.scipy.linalg.solve_triangular(lower, sketch.T, lower=True).T


def region_tables(block_regions, region_mask, region_in, region_out):
    regions = region_mask.shape[0]
    signal_width = region_in.shape[1]
    block_total = block_regions.shape[0]
    block_rows = region_in.shape[0] // block_total
    onehot = (block_regions[:, None] == jnp.arange(regions, dtype=jnp.int32)[None, :]).astype(
        jnp.float32
    )
    onehot = jnp.broadcast_to(onehot[:, None, :], (block_total, block_rows, regions)).reshape(
        block_total * block_rows, regions
    )
    allowed = jnp.dot(onehot, region_mask.astype(jnp.float32), precision=precise)
    region_feed = (onehot[:, :, None] * region_in.astype(jnp.float32)[:, None, :]).reshape(
        -1, regions * signal_width
    )
    spread = (allowed[:, :, None] * region_out.astype(jnp.float32)[:, None, :]).reshape(
        -1, regions * signal_width
    )
    return (region_feed.astype(jnp.bfloat16), spread.astype(jnp.bfloat16))


def local(
    activity,
    test_matrix,
    basis_mix,
    recurrent,
    latent_bias,
    readout,
    region_in,
    region_out,
    region_of_block,
    region_mask,
):
    neurons_here, frames_here = activity.shape
    contract = (((0,), (0,)), ((), ()))
    block_count = neurons_here // BLOCK
    my_blocks = lax.dynamic_slice_in_dim(
        region_of_block, lax.axis_index("region") * block_count, block_count
    )
    region_feed, spread = region_tables(my_blocks, region_mask, region_in, region_out)
    test_full = lax.all_gather(test_matrix, "region", axis=1, tiled=True)
    sketch_rows = lax.psum_scatter(
        jnp.dot(activity, test_full, preferred_element_type=jnp.float32),
        "tm",
        scatter_dimension=0,
        tiled=True,
    )
    gram = lax.psum(jnp.dot(sketch_rows.T, sketch_rows, precision=precise), ("tm", "region"))
    loading_rows = jnp.dot(orthonormal(sketch_rows, gram), basis_mix, precision=precise).astype(
        jnp.bfloat16
    )
    latent_part = lax.dot_general(
        lax.all_gather(loading_rows, "tm", axis=0, tiled=True),
        activity,
        contract,
        preferred_element_type=jnp.float32,
    )
    signal_part = lax.dot_general(
        region_feed, activity, contract, preferred_element_type=jnp.float32
    )
    latents, signals = lax.psum((latent_part, signal_part), "region")
    prior_latent, prior_signal = from_behind((latents[:, -1:], signals[:, -1:]), "tm", 1)
    lagged_latents = jnp.concatenate([prior_latent, latents[:, :-1]], axis=1)
    lagged_signals = jnp.concatenate([prior_signal, signals[:, :-1]], axis=1)
    hidden = jnp.tanh(jnp.dot(recurrent, lagged_latents, precision=precise) + latent_bias[:, None])
    predicted = jnp.dot(readout, hidden.astype(jnp.bfloat16), preferred_element_type=jnp.float32)
    predicted = predicted + jnp.dot(
        spread, lagged_signals.astype(jnp.bfloat16), preferred_element_type=jnp.float32
    )
    error = activity.astype(jnp.float32) - predicted
    squared = error * error
    cross, error_sq, hidden_sq = lax.psum(
        (
            jnp.dot(error, hidden.T, precision=precise),
            jnp.sum(squared, axis=1),
            jnp.sum(hidden * hidden, axis=1),
        ),
        "tm",
    )
    frame_sq = lax.psum(jnp.sum(squared, axis=0), "region")
    frames_all = frames_here * lax.axis_size("tm")
    frame_loss = frame_sq / (neurons_here * lax.axis_size("region"))
    readout_score = cross / jnp.sqrt(
        frames_all
        * (error_sq[:, None] / frames_all + epsilon)
        * (hidden_sq[None, :] / frames_all + epsilon)
    )
    return (latents, frame_loss, readout_score)


def solution(mesh):
    in_specs = (
        P("region", "tm"),
        P("tm", "region"),
        P(),
        P(),
        P(),
        P("region", None),
        P("region", None),
        P("region", None),
        P(),
        P(),
    )
    out_specs = (P(None, "tm"), P("tm"), P("region", None))
    return jax.shard_map(local, mesh=mesh, in_specs=in_specs, out_specs=out_specs, check_vma=False)
```

profile of v0, /device:TPU:8, one launch (start us, length us, event | category | flops | bytes accessed | tf_op | source)
XLA Modules:
  0.0 1049.4 jit_solution(13345600834286897948)
XLA Ops:
  8.0 50.1 %all-gather.3.cloned.1.call-done = bf16[2048,512]{0,1:T(8,128)(2,1)} async-done(((bf16[2048,64]{0,1:T(8,128)(2,1)}), bf16[2048,512]{0,1:T(8,128)(2,1)}) %all-gather.3.cloned.1.call-update) | async-done | bytes 2097168 | tf_op jit(solution)/shard_map/all_gather | solution.py:62
  58.1 5.5 fusion.73
  63.6 141.2 %fusion = f32[16,512]{1,0:T(8,128)S(1)} fusion(f32[768,512]{1,0:T(8,128)} %fusion.73), kind=kCustom, calls=%all-reduce-scatter | all-reduce-scatter fusion | flops 524289 | bytes 1607680
  212.7 11.6 %collective-permute-start.11 = (f32[16,512]{1,0:T(8,128)S(1)}, f32[16,512]{1,0:T(8,128)S(1)}, u32[]{:S(2)}, u32[]{:S(2)}) collective-permute-start(f32[16,512]{1,0:T(8,128)S(1)} %fusion), channel_id=1, source_target_pairs={{0,80},{8,88},{16,96},{24,104},{32,112},{40,120},{48,128},{56,136}... | collective-permute-start | bytes 98312
  226.3 5.7 collective-permute-start.9
  237.3 4.1 collective-permute-start.6
  254.9 23.2 %concatenate.21 = f32[268,512]{1,0:T(8,128)} concatenate(f32[12,512]{1,0:T(8,128)S(1)} %collective-permute-done.17, f32[16,512]{1,0:T(8,128)S(1)} %collective-permute-done.16, f32[16,512]{1,0:T(8,128)S(1)} %collective-permute-done.15, f32[16,512]{1,0:T(8,128)S(1)} %collective-permute-done.14, f32[16,512]{1,0:T(8,128)S(1)} %collective-permute-done.13, ...), dimensions={0} | concatenate | bytes 1097728
  284.4 262.1 %all-reduce.9.cloned.1.call-done = f32[512,512]{0,1:T(8,128)} async-done(((f32[512,512]{0,1:T(8,128)}), f32[512,512]{0,1:T(8,128)}) %all-reduce.9.cloned.1.call-update) | async-done | bytes 1048592 | tf_op jit(solution)/shard_map/psum | solution.py:69
  551.8 11.7 %cholesky.104 = f32[128,128]{1,0:T(8,128)S(1)} custom-call(f32[128,128]{1,0:T(8,128)S(1)} %cholesky.266), custom_call_target="Cholesky" | custom-call | tf_op jit(solution)/shard_map/jit(cholesky)/cholesky | solution.py:18
  563.6 9.8 custom-call.31
  578.4 12.5 %cholesky.217 = f32[128,128]{1,0:T(8,128)S(1)} custom-call(f32[128,128]{1,0:T(8,128)} %cholesky.270), custom_call_target="Cholesky" | custom-call | tf_op jit(solution)/shard_map/jit(cholesky)/cholesky | solution.py:18
  591.6 10.8 %custom-call.32 = f32[1,128,128]{1,2,0:T(8,128)S(1)} custom-call(f32[1,128,128]{2,1,0:T(8,128)} %get-tuple-element.31), custom_call_target="InvertDiagBlocksLowerTriangular" | custom-call | tf_op jit(solution)/shard_map/jit(cholesky)/cholesky | solution.py:18
  604.8 11.7 %cholesky.238 = f32[128,128]{1,0:T(8,128)S(1)} custom-call(f32[128,128]{1,0:T(8,128)S(1)} %cholesky.275), custom_call_target="Cholesky" | custom-call | tf_op jit(solution)/shard_map/jit(cholesky)/cholesky | solution.py:18
  617.8 9.8 custom-call.33
  629.9 11.9 %cholesky.255 = f32[128,128]{1,0:T(8,128)S(1)} custom-call(f32[128,128]{1,0:T(8,128)S(1)} %convolution_subtract_fusion.2), custom_call_target="Cholesky" | custom-call | tf_op jit(solution)/shard_map/jit(cholesky)/cholesky | solution.py:18
  648.6 14.4 %while.1 = (s32[]{:T(128)}, f32[512,512]{1,0:T(8,128)}, s32[4,2]{0,1:T(2,128)S(1)}, f32[4,128,128]{2,1,0:T(8,128)}, s32[]{:T(128)}) while((s32[]{:T(128)}, f32[512,512]{1,0:T(8,128)}, s32[4,2]{0,1:T(2,128)S(1)}, f32[4,128,128]{2,1,0:T(8,128)}, s32[]{:T(128)}) %tuple.34), condition=%wide.while_cond, body=%wide.while_body.sunk | while | flops 2 | bytes 132205 | solution.py:19
  663.0 40.1 %custom-call.34 = f32[4,128,128]{1,2,0:T(8,128)S(1)} custom-call(f32[4,128,128]{2,1,0:T(8,128)} %get-tuple-element.10), custom_call_target="InvertDiagBlocksLowerTriangular" | custom-call | tf_op jit(solution)/shard_map/jit(_solve_triangular)/triangular_solve | solution.py:19
  710.3 43.1 %all-gather = bf16[64,12,64]{2,1,0:T(8,128)(2,1)S(1)} all-gather(bf16[1,12,64]{2,1,0:T(8,128)(2,1)S(1)} %fusion.3), channel_id=1, replica_groups=mesh['tm'=64,'region'=8] {'tm'}, dimensions={0}, use_global_device_ids=true | all-gather | bytes 99840 | tf_op jit(solution)/shard_map/all_gather | solution.py:74
  756.7 35.5 %all-reduce.14 = bf16[64,2048]{1,0:T(8,128)(2,1)S(1)} all-reduce(f32[64,2048]{1,0:T(8,128)} %fusion.26), channel_id=1, replica_groups=mesh['tm'=64,'region'=8] {'region'}, use_global_device_ids=true, to_apply=%region_11.12 | all-reduce | flops 131072 | bytes 786432 | tf_op jit(solution)/shard_map/psum | solution.py:82
  794.7 36.6 %all-reduce.11.cloned.1.call-done = f32[64,2048]{1,0:T(8,128)} async-done(((f32[64,2048]{1,0:T(8,128)}), f32[64,2048]{1,0:T(8,128)}) %all-reduce.11.cloned.1.call-update) | async-done | bytes 524304 | tf_op jit(solution)/shard_map/psum | solution.py:82
  845.2 4.8 fusion.75
  850.0 129.4 %all-reduce.3 = (f32[64]{0:T(128)S(1)}, f32[768]{0:T(1024)S(1)}) all-reduce(f32[64]{0:T(128)S(1)} %get-tuple-element.38, f32[768]{0:T(1024)S(1)} %get-tuple-element.11), channel_id=1, replica_groups=mesh['tm'=64,'region'=8] {'tm'}, use_global_device_ids=true, to_apply=%region_18.19 | all-reduce | flops 832 | bytes 6656 | tf_op jit(solution)/shard_map/psum | solution.py:93
  979.4 15.0 %psum.52 = f32[2048]{0:T(1024)S(1)} all-reduce(f32[2048]{0:T(1024)S(1)} %get-tuple-element.12), channel_id=1, replica_groups=mesh['tm'=64,'region'=8] {'region'}, use_global_device_ids=true, to_apply=%region_13.14 | all-reduce | flops 2048 | bytes 16384 | tf_op jit(solution)/shard_map/psum | solution.py:101
  995.0 45.1 %all-reduce.13.cloned.1.call-done = f32[768,64]{0,1:T(8,128)} async-done(((f32[768,64]{0,1:T(8,128)}), f32[768,64]{0,1:T(8,128)}) %all-reduce.13.cloned.1.call-update) | async-done | bytes 196624 | tf_op jit(solution)/shard_map/psum | solution.py:93
  (142 shorter events, 100.4 us)
Async XLA Ops:
  7.2 702.9 %copy-start = (f32[512,64]{0,1:T(8,128)S(1)}, f32[512,64]{0,1:T(8,128)}, u32[]{:S(2)}) copy-start(f32[512,64]{0,1:T(8,128)} %param.12) | copy-start | bytes 393220
  7.2 50.9 %all-gather.3.cloned.1.call-start = ((), (), s32[]{:S(2)}) async-start(), calls=%async_computation | async-start | bytes 2359296 | tf_op jit(solution)/shard_map/all_gather | solution.py:62
  7.9 538.6 %all-reduce.9.cloned.1.call-start = ((), (), s32[]{:S(2)}) async-start(), calls=%async_computation.1 | async-start | bytes 2097152 | tf_op jit(solution)/shard_map/psum | solution.py:69
  63.6 218.0 %copy-start.1 = (bf16[768,2048]{1,0:T(8,128)(2,1)S(1)}, bf16[768,2048]{1,0:T(8,128)(2,1)}, u32[]{:S(2)}) copy-start(bf16[768,2048]{1,0:T(8,128)(2,1)} %param.10) | copy-start | bytes 9437188
  204.8 6.5 collective-permute-start.17
  206.1 6.6 collective-permute-start.16
  207.4 16.9 %collective-permute-start.15 = (f32[16,512]{1,0:T(8,128)S(1)}, f32[16,512]{1,0:T(8,128)S(1)}, u32[]{:S(2)}, u32[]{:S(2)}) collective-permute-start(f32[16,512]{1,0:T(8,128)S(1)} %fusion), channel_id=1, source_target_pairs={{0,112},{8,120},{16,128},{24,136},{32,144},{40,152},{48,160},{56,1... | collective-permute-start | bytes 98312
  208.7 17.5 %collective-permute-start.14 = (f32[16,512]{1,0:T(8,128)S(1)}, f32[16,512]{1,0:T(8,128)S(1)}, u32[]{:S(2)}, u32[]{:S(2)}) collective-permute-start(f32[16,512]{1,0:T(8,128)S(1)} %fusion), channel_id=1, source_target_pairs={{0,104},{8,112},{16,120},{24,128},{32,136},{40,144},{48,152},{56,1... | collective-permute-start | bytes 98312
  210.0 21.9 %collective-permute-start.13 = (f32[16,512]{1,0:T(8,128)S(1)}, f32[16,512]{1,0:T(8,128)S(1)}, u32[]{:S(2)}, u32[]{:S(2)}) collective-permute-start(f32[16,512]{1,0:T(8,128)S(1)} %fusion), channel_id=1, source_target_pairs={{0,96},{8,104},{16,112},{24,120},{32,128},{40,136},{48,144},{56,15... | collective-permute-start | bytes 98312
  211.3 22.1 %collective-permute-start.12 = (f32[16,512]{1,0:T(8,128)S(1)}, f32[16,512]{1,0:T(8,128)S(1)}, u32[]{:S(2)}, u32[]{:S(2)}) collective-permute-start(f32[16,512]{1,0:T(8,128)S(1)} %fusion), channel_id=1, source_target_pairs={{0,88},{8,96},{16,104},{24,112},{32,120},{40,128},{48,136},{56,144... | collective-permute-start | bytes 98312
  212.7 24.6 %collective-permute-start.11 = (f32[16,512]{1,0:T(8,128)S(1)}, f32[16,512]{1,0:T(8,128)S(1)}, u32[]{:S(2)}, u32[]{:S(2)}) collective-permute-start(f32[16,512]{1,0:T(8,128)S(1)} %fusion), channel_id=1, source_target_pairs={{0,80},{8,88},{16,96},{24,104},{32,112},{40,120},{48,128},{56,136}... | collective-permute-start | bytes 98312
  224.3 17.2 %collective-permute-start.10 = (f32[16,512]{1,0:T(8,128)S(1)}, f32[16,512]{1,0:T(8,128)S(1)}, u32[]{:S(2)}, u32[]{:S(2)}) collective-permute-start(f32[16,512]{1,0:T(8,128)S(1)} %fusion), channel_id=1, source_target_pairs={{0,72},{8,80},{16,88},{24,96},{32,104},{40,112},{48,120},{56,128},... | collective-permute-start | bytes 98312
  226.3 18.6 %collective-permute-start.9 = (f32[16,512]{1,0:T(8,128)S(1)}, f32[16,512]{1,0:T(8,128)S(1)}, u32[]{:S(2)}, u32[]{:S(2)}) collective-permute-start(f32[16,512]{1,0:T(8,128)S(1)} %fusion), channel_id=1, source_target_pairs={{0,64},{8,72},{16,80},{24,88},{32,96},{40,104},{48,112},{56,120},{... | collective-permute-start | bytes 98312
  231.9 15.6 %collective-permute-start.8 = (f32[16,512]{1,0:T(8,128)S(1)}, f32[16,512]{1,0:T(8,128)S(1)}, u32[]{:S(2)}, u32[]{:S(2)}) collective-permute-start(f32[16,512]{1,0:T(8,128)S(1)} %fusion), channel_id=1, source_target_pairs={{0,56},{8,64},{16,72},{24,80},{32,88},{40,96},{48,104},{56,112},{6... | collective-permute-start | bytes 98312
  233.4 16.7 %collective-permute-start.7 = (f32[16,512]{1,0:T(8,128)S(1)}, f32[16,512]{1,0:T(8,128)S(1)}, u32[]{:S(2)}, u32[]{:S(2)}) collective-permute-start(f32[16,512]{1,0:T(8,128)S(1)} %fusion), channel_id=1, source_target_pairs={{0,48},{8,56},{16,64},{24,72},{32,80},{40,88},{48,96},{56,104},{64... | collective-permute-start | bytes 98312
  237.3 17.5 %collective-permute-start.6 = (f32[16,512]{1,0:T(8,128)S(1)}, f32[16,512]{1,0:T(8,128)}, u32[]{:S(2)}, u32[]{:S(2)}) collective-permute-start(f32[16,512]{1,0:T(8,128)S(1)} %fusion), channel_id=1, source_target_pairs={{0,40},{8,48},{16,56},{24,64},{32,72},{40,80},{48,88},{56,96},{64,... | collective-permute-start | bytes 98312
  241.5 13.4 %collective-permute-start.5 = (f32[16,512]{1,0:T(8,128)S(1)}, f32[16,512]{1,0:T(8,128)}, u32[]{:S(2)}, u32[]{:S(2)}) collective-permute-start(f32[16,512]{1,0:T(8,128)S(1)} %fusion), channel_id=1, source_target_pairs={{0,32},{8,40},{16,48},{24,56},{32,64},{40,72},{48,80},{56,88},{64,... | collective-permute-start | bytes 98312
  244.8 10.1 collective-permute-start.4
  247.5 7.4 collective-permute-start.3
  250.1 4.8 collective-permute-start.2
  281.0 550.3 %all-reduce.11.cloned.1.call-start = ((), (), s32[]{:S(2)}) async-start(), calls=%async_computation.2 | async-start | bytes 1048576 | tf_op jit(solution)/shard_map/psum | solution.py:82
  756.6 283.5 %all-reduce.13.cloned.1.call-start = ((), (), s32[]{:S(2)}) async-start(), calls=%async_computation.3 | async-start | bytes 393216 | tf_op jit(solution)/shard_map/psum | solution.py:93
  792.8 49.8 %collective-permute-start.1 = (bf16[64,1]{1,0:T(8,128)(2,1)}, bf16[64,1]{1,0:T(8,128)(2,1)}, u32[]{:S(2)}, u32[]{:S(2)}) collective-permute-start(bf16[64,1]{1,0:T(8,128)(2,1)} %slice.144), channel_id=1, source_target_pairs={{0,8},{8,16},{16,24},{24,32},{32,40},{40,48},{48,56},{56,64},{64,7... | collective-permute-start | bytes 392 | tf_op jit(solution)/shard_map/ppermute | solution.py:14
  832.7 5.8 collective-permute-start
  (15 other events, 716.0 us)
Sparse Core Ops, SparseCore 0:
  10.1 47.9 all-gather.2
  281.1 265.3 all-reduce.8
  756.7 74.5 all-reduce.10
  850.1 189.9 all-reduce.12
where the time goes:
time: 1060 us; the launch traced here: 1050 us
  waiting for transfers between devices  395 us (37%)
  blocking collectives  364 us (34%)
  other arithmetic  130 us (12%)
  local copies, waits for them, and re-layouts  52.3 us (5%)
  starting transfers between devices  51.6 us (5%)
  matrix products  39.4 us (4%)
  between operations  17.7 us (2%)
    psum x1, waiting for transfers between devices, local(): lax.psum(jnp.dot(sketch_rows.T, sketch_rows, precision=precise), ('tm', '...  262 us
    unnamed x1, blocking collectives  141 us
    psum x1, blocking collectives, local(): lax.psum((jnp.dot(error, hidden.T, precision=precise), jnp.sum(squared, a...  129 us
    another operation x14, other arithmetic, orthonormal(): lower = jnp.linalg.cholesky(gram)  82.2 us
    all_gather x1, waiting for transfers between devices, local(): test_full = lax.all_gather(test_matrix, 'region', axis=1, tiled=True)  50.1 us
    unnamed x16, starting transfers between devices  47 us
    psum x1, waiting for transfers between devices, local(): lax.psum((jnp.dot(error, hidden.T, precision=precise), jnp.sum(squared, a...  45.1 us
    all_gather x1, blocking collectives, local(): lax.all_gather(loading_rows, 'tm', axis=0, tiled=True)  43.1 us
  transfers between devices with their start and end apart: 22, of which 4 were waited for; matrix products, arithmetic and copies ran while one was open for 1% of the time, Pallas kernels for 0%

commit v1 on v0

--- a/solution.py
+++ b/solution.py
@@ -59,7 +59,18 @@
         region_of_block, lax.axis_index("region") * block_count, block_count
     )
     region_feed, spread = region_tables(my_blocks, region_mask, region_in, region_out)
-    test_full = lax.all_gather(test_matrix, "region", axis=1, tiled=True)
+    size, place, rows = (lax.axis_size("region"), lax.axis_index("region"), test_matrix.shape[1])
+    upward = [(i_2, (i_2 + 1) % size) for i_2 in range(size)]
+    out = jnp.zeros(
+        (*test_matrix.shape[:1], size * rows, *test_matrix.shape[1 + 1 :]), test_matrix.dtype
+    )
+    block_2 = test_matrix
+    for hop in range(size):
+        owner = (place - hop) % size
+        out = lax.dynamic_update_slice_in_dim(out, block_2, owner * rows, axis=1)
+        if hop < size - 1:
+            block_2 = lax.ppermute(block_2, "region", upward)
+    test_full = out
     sketch_rows = lax.psum_scatter(
         jnp.dot(activity, test_full, preferred_element_type=jnp.float32),
         "tm",

time: 1060 us -> 1070 us (level)
  waiting for transfers between devices: 395 us -> 605 us
  blocking collectives: 364 us -> 223 us
  starting transfers between devices: 51.6 us -> 19.7 us
  local copies, waits for them, and re-layouts: 52.3 us -> 34.1 us
    unnamed x20 -> x5, waiting for transfers between devices: 0.77 us -> 196 us
    unnamed x1 -> x0, blocking collectives: 141 us -> none
    ppermute x0 -> x7, waiting for transfers between devices: none -> 59.3 us  [local(): block_2 = lax.ppermute(block_2, 'region', upward)]
    all_gather x1 -> x0, waiting for transfers between devices: 50.1 us -> none  [local(): test_full = lax.all_gather(test_matrix, 'region', axis=1, tiled=True)]
    unnamed x16 -> x1, starting transfers between devices: 47 us -> 0.04 us
    unnamed x40 -> x37, local copies, waits for them, and re-layouts: 29.9 us -> 9.26 us
    ppermute x0 -> x7, starting transfers between devices: none -> 15.1 us  [local(): block_2 = lax.ppermute(block_2, 'region', upward)]
  transfers between devices with their start and end apart: 22 -> 13, of which waited for: 4 -> 11; matrix products, arithmetic and copies ran while one was open for 1% -> 2% of each run, Pallas kernels for 0% -> 0%
where the time goes in v1:
time: 1070 us; the launch traced here: 1060 us
  waiting for transfers between devices  605 us (57%)
  blocking collectives  223 us (21%)
  other arithmetic  129 us (12%)
  matrix products  34.7 us (3%)
  local copies, waits for them, and re-layouts  34.1 us (3%)
  starting transfers between devices  19.7 us (2%)
  between operations  17.8 us (2%)
    psum x1, waiting for transfers between devices, local(): lax.psum(jnp.dot(sketch_rows.T, sketch_rows, precision=precise), ('tm', '...  268 us
    unnamed x5, waiting for transfers between devices  196 us
    psum x1, blocking collectives, local(): lax.psum((jnp.dot(error, hidden.T, precision=precise), jnp.sum(squared, a...  129 us
    another operation x14, other arithmetic, orthonormal(): lower = jnp.linalg.cholesky(gram)  82.2 us
    ppermute x7, waiting for transfers between devices, local(): block_2 = lax.ppermute(block_2, 'region', upward)  59.3 us
    psum x1, waiting for transfers between devices, local(): lax.psum((jnp.dot(error, hidden.T, precision=precise), jnp.sum(squared, a...  45.1 us
    all_gather x1, blocking collectives, local(): lax.all_gather(loading_rows, 'tm', axis=0, tiled=True)  43.1 us
    another operation x3, other arithmetic, orthonormal(): return jax.scipy.linalg.solve_triangular(lower, sketch.T, lower=True).T  42.5 us
  transfers between devices with their start and end apart: 13, of which 11 were waited for; matrix products, arithmetic and copies ran while one was open for 2% of the time, Pallas kernels for 0%

profile of v1, /device:TPU:8, one launch (start us, length us, event | category | flops | bytes accessed | tf_op | source)
XLA Modules:
  0.0 1063.5 jit_solution(10137348709128261745)
XLA Ops:
  10.9 8.8 collective-permute-done
  22.3 7.5 collective-permute-done.1
  32.4 9.1 collective-permute-done.2
  43.9 10.2 collective-permute-done.3
  56.1 10.0 collective-permute-done.4
  70.0 6.5 collective-permute-done.5
  78.4 7.2 collective-permute-done.6
  90.9 196.0 %all-reduce.15.cloned.1.call-done = f32[768,512]{0,1:T(8,128)} async-done(((f32[768,512]{0,1:T(8,128)}), f32[768,512]{0,1:T(8,128)}) %all-reduce.15.cloned.1.call-update) | async-done | bytes 1572880
  294.3 268.2 %all-reduce.9.cloned.1.call-done = f32[512,512]{0,1:T(8,128)} async-done(((f32[512,512]{0,1:T(8,128)}), f32[512,512]{0,1:T(8,128)}) %all-reduce.9.cloned.1.call-update) | async-done | bytes 1048592 | tf_op jit(solution)/shard_map/psum | solution.py:80
  567.9 11.7 %cholesky.104 = f32[128,128]{1,0:T(8,128)S(1)} custom-call(f32[128,128]{1,0:T(8,128)S(1)} %cholesky.266), custom_call_target="Cholesky" | custom-call | tf_op jit(solution)/shard_map/jit(cholesky)/cholesky | solution.py:18
  579.6 9.8 custom-call.31
  594.5 12.5 %cholesky.217 = f32[128,128]{1,0:T(8,128)S(1)} custom-call(f32[128,128]{1,0:T(8,128)} %cholesky.270), custom_call_target="Cholesky" | custom-call | tf_op jit(solution)/shard_map/jit(cholesky)/cholesky | solution.py:18
  607.7 10.8 %custom-call.32 = f32[1,128,128]{1,2,0:T(8,128)S(1)} custom-call(f32[1,128,128]{2,1,0:T(8,128)} %get-tuple-element.31), custom_call_target="InvertDiagBlocksLowerTriangular" | custom-call | tf_op jit(solution)/shard_map/jit(cholesky)/cholesky | solution.py:18
  620.9 11.7 %cholesky.238 = f32[128,128]{1,0:T(8,128)S(1)} custom-call(f32[128,128]{1,0:T(8,128)S(1)} %cholesky.275), custom_call_target="Cholesky" | custom-call | tf_op jit(solution)/shard_map/jit(cholesky)/cholesky | solution.py:18
  633.9 9.8 custom-call.33
  645.9 11.9 %cholesky.255 = f32[128,128]{1,0:T(8,128)S(1)} custom-call(f32[128,128]{1,0:T(8,128)S(1)} %convolution_subtract_fusion.2), custom_call_target="Cholesky" | custom-call | tf_op jit(solution)/shard_map/jit(cholesky)/cholesky | solution.py:18
  664.6 14.5 %while.1 = (s32[]{:T(128)}, f32[512,512]{1,0:T(8,128)}, s32[4,2]{0,1:T(2,128)S(1)}, f32[4,128,128]{2,1,0:T(8,128)}, s32[]{:T(128)}) while((s32[]{:T(128)}, f32[512,512]{1,0:T(8,128)}, s32[4,2]{0,1:T(2,128)S(1)}, f32[4,128,128]{2,1,0:T(8,128)}, s32[]{:T(128)}) %tuple.34), condition=%wide.while_cond, body=%wide.while_body.sunk | while | flops 2 | bytes 132205 | solution.py:19
  679.1 40.1 %custom-call.34 = f32[4,128,128]{1,2,0:T(8,128)S(1)} custom-call(f32[4,128,128]{2,1,0:T(8,128)} %get-tuple-element.10), custom_call_target="InvertDiagBlocksLowerTriangular" | custom-call | tf_op jit(solution)/shard_map/jit(_solve_triangular)/triangular_solve | solution.py:19
  724.3 43.1 %all-gather = bf16[64,12,64]{2,1,0:T(8,128)(2,1)S(1)} all-gather(bf16[1,12,64]{2,1,0:T(8,128)(2,1)S(1)} %fusion.2), channel_id=1, replica_groups=mesh['tm'=64,'region'=8] {'tm'}, dimensions={0}, use_global_device_ids=true | all-gather | bytes 99840 | tf_op jit(solution)/shard_map/all_gather | solution.py:85
  770.7 35.5 %all-reduce.16 = bf16[64,2048]{1,0:T(8,128)(2,1)S(1)} all-reduce(f32[64,2048]{1,0:T(8,128)} %fusion.23), channel_id=1, replica_groups=mesh['tm'=64,'region'=8] {'region'}, use_global_device_ids=true, to_apply=%region_11.12 | all-reduce | flops 131072 | bytes 786432 | tf_op jit(solution)/shard_map/psum | solution.py:93
  808.8 36.6 %all-reduce.11.cloned.1.call-done = f32[64,2048]{1,0:T(8,128)} async-done(((f32[64,2048]{1,0:T(8,128)}), f32[64,2048]{1,0:T(8,128)}) %all-reduce.11.cloned.1.call-update) | async-done | bytes 524304 | tf_op jit(solution)/shard_map/psum | solution.py:93
  864.0 129.4 %all-reduce.2 = (f32[64]{0:T(128)S(1)}, f32[768]{0:T(1024)S(1)}) all-reduce(f32[64]{0:T(128)S(1)} %get-tuple-element.38, f32[768]{0:T(1024)S(1)} %get-tuple-element.11), channel_id=1, replica_groups=mesh['tm'=64,'region'=8] {'tm'}, use_global_device_ids=true, to_apply=%region_18.19 | all-reduce | flops 832 | bytes 6656 | tf_op jit(solution)/shard_map/psum | solution.py:104
  993.5 15.0 %psum.52 = f32[2048]{0:T(1024)S(1)} all-reduce(f32[2048]{0:T(1024)S(1)} %get-tuple-element.12), channel_id=1, replica_groups=mesh['tm'=64,'region'=8] {'region'}, use_global_device_ids=true, to_apply=%region_13.14 | all-reduce | flops 2048 | bytes 16384 | tf_op jit(solution)/shard_map/psum | solution.py:112
  1009.0 45.1 %all-reduce.13.cloned.1.call-done = f32[768,64]{0,1:T(8,128)} async-done(((f32[768,64]{0,1:T(8,128)}), f32[768,64]{0,1:T(8,128)}) %all-reduce.13.cloned.1.call-update) | async-done | bytes 196624 | tf_op jit(solution)/shard_map/psum | solution.py:104
  (129 shorter events, 99.1 us)
Async XLA Ops:
  7.2 716.9 %copy-start = (f32[512,64]{0,1:T(8,128)S(1)}, f32[512,64]{0,1:T(8,128)}, u32[]{:S(2)}) copy-start(f32[512,64]{0,1:T(8,128)} %param.12) | copy-start | bytes 393220
  7.2 36.7 %copy-start.5 = (bf16[2048,64]{0,1:T(8,128)(2,1)S(1)}, bf16[2048,64]{0,1:T(8,128)(2,1)}, u32[]{:S(2)}) copy-start(bf16[2048,64]{0,1:T(8,128)(2,1)} %param.11) | copy-start | bytes 786436
  7.2 279.7 %all-reduce.15.cloned.1.call-start = ((), (), s32[]{:S(2)}) async-start(), calls=%async_computation.3 | async-start | bytes 3145728
  7.2 12.4 %collective-permute-start = (bf16[2048,64]{0,1:T(8,128)(2,1)}, bf16[2048,64]{0,1:T(8,128)(2,1)S(1)}, u32[]{:S(2)}, u32[]{:S(2)}) collective-permute-start(bf16[2048,64]{0,1:T(8,128)(2,1)} %param.11), channel_id=1, source_target_pairs={{0,1},{1,2},{2,3},{3,4},{4,5},{5,6},{6,7},{7,0},{8,9},{9,10},{10,1... | collective-permute-start | bytes 786440 | tf_op jit(solution)/shard_map/ppermute | solution.py:72
  20.4 9.5 collective-permute-start.1
  30.5 11.0 %collective-permute-start.2 = (bf16[2048,64]{0,1:T(8,128)(2,1)S(1)}, bf16[2048,64]{0,1:T(8,128)(2,1)}, u32[]{:S(2)}, u32[]{:S(2)}) collective-permute-start(bf16[2048,64]{0,1:T(8,128)(2,1)S(1)} %collective-permute-done.1), channel_id=1, source_target_pairs={{0,1},{1,2},{2,3},{3,4},{4,5},{5,6},{6,7},{7,0},{8,9},{9,10},{10,1... | collective-permute-start | bytes 786440 | tf_op jit(solution)/shard_map/ppermute | solution.py:72
  41.5 12.6 %collective-permute-start.3 = (bf16[2048,64]{0,1:T(8,128)(2,1)}, bf16[2048,64]{0,1:T(8,128)(2,1)}, u32[]{:S(2)}, u32[]{:S(2)}) collective-permute-start(bf16[2048,64]{0,1:T(8,128)(2,1)} %collective-permute-done.2), channel_id=1, source_target_pairs={{0,1},{1,2},{2,3},{3,4},{4,5},{5,6},{6,7},{7,0},{8,9},{9,10},{10,1... | collective-permute-start | bytes 786440 | tf_op jit(solution)/shard_map/ppermute | solution.py:72
  43.6 12.4 %copy-start.7 = (bf16[2048,64]{0,1:T(8,128)(2,1)S(1)}, bf16[2048,64]{0,1:T(8,128)(2,1)}, u32[]{:S(2)}) copy-start(bf16[2048,64]{0,1:T(8,128)(2,1)} %copy-done.6) | copy-start | bytes 786436
  43.6 12.5 %copy-start.9 = (bf16[2048,64]{0,1:T(8,128)(2,1)S(1)}, bf16[2048,64]{0,1:T(8,128)(2,1)}, u32[]{:S(2)}) copy-start(bf16[2048,64]{0,1:T(8,128)(2,1)} %copy-done.8) | copy-start | bytes 786436
  43.9 41.8 %copy-start.1 = (bf16[768,2048]{1,0:T(8,128)(2,1)S(1)}, bf16[768,2048]{1,0:T(8,128)(2,1)}, u32[]{:S(2)}) copy-start(bf16[768,2048]{1,0:T(8,128)(2,1)} %param.10) | copy-start | bytes 9437188
  54.1 12.0 %collective-permute-start.4 = (bf16[2048,64]{0,1:T(8,128)(2,1)}, bf16[2048,64]{0,1:T(8,128)(2,1)S(1)}, u32[]{:S(2)}, u32[]{:S(2)}) collective-permute-start(bf16[2048,64]{0,1:T(8,128)(2,1)} %collective-permute-done.3), channel_id=1, source_target_pairs={{0,1},{1,2},{2,3},{3,4},{4,5},{5,6},{6,7},{7,0},{8,9},{9,10},{10,1... | collective-permute-start | bytes 786440 | tf_op jit(solution)/shard_map/ppermute | solution.py:72
  66.1 10.3 collective-permute-start.5
  76.4 9.2 collective-permute-start.6
  85.7 5.1 copy-start.15
  88.7 202.6 %copy-start.11 = (bf16[768,8]{0,1:T(8,128)(2,1)S(1)}, bf16[768,8]{0,1:T(8,128)(2,1)}, u32[]{:S(2)}) copy-start(bf16[768,8]{0,1:T(8,128)(2,1)} %param.16) | copy-start | bytes 36868
  88.8 473.8 %all-reduce.9.cloned.1.call-start = ((), (), s32[]{:S(2)}) async-start(), calls=%async_computation | async-start | bytes 2097152 | tf_op jit(solution)/shard_map/psum | solution.py:80
  290.2 555.2 %all-reduce.11.cloned.1.call-start = ((), (), s32[]{:S(2)}) async-start(), calls=%async_computation.1 | async-start | bytes 1048576 | tf_op jit(solution)/shard_map/psum | solution.py:93
  768.2 80.7 %copy-start.14 = (s32[8,8]{1,0:T(8,128)S(1)}, s32[8,8]{1,0:T(8,128)}, u32[]{:S(2)}) copy-start(s32[8,8]{1,0:T(8,128)} %param.19) | copy-start | bytes 772
  770.6 283.5 %all-reduce.13.cloned.1.call-start = ((), (), s32[]{:S(2)}) async-start(), calls=%async_computation.2 | async-start | bytes 393216 | tf_op jit(solution)/shard_map/psum | solution.py:104
  806.9 49.8 %collective-permute-start.8 = (bf16[64,1]{1,0:T(8,128)(2,1)}, bf16[64,1]{1,0:T(8,128)(2,1)}, u32[]{:S(2)}, u32[]{:S(2)}) collective-permute-start(bf16[64,1]{1,0:T(8,128)(2,1)} %slice.144), channel_id=1, source_target_pairs={{0,8},{8,16},{16,24},{24,32},{32,40},{40,48},{48,56},{56,64},{64,7... | collective-permute-start | bytes 392 | tf_op jit(solution)/shard_map/ppermute | solution.py:14
  846.8 5.8 collective-permute-start.7
  849.8 2.8 copy-start.12
  849.8 2.8 copy-start.13
  859.2 196.7 %copy-start.4 = (f32[64,2048]{1,0:T(8,128)S(1)}, f32[64,2048]{1,0:T(8,128)}, u32[]{:S(2)}) copy-start(f32[64,2048]{1,0:T(8,128)} %all-reduce.11.cloned.1.call-done) | copy-start | bytes 1572868
  (5 other events, 6.6 us)
Sparse Core Ops, SparseCore 0:
  88.9 197.9 all-reduce.14
  292.0 270.4 all-reduce.8
  770.8 74.5 all-reduce.10
  864.2 189.9 all-reduce.12
